TPU v7x, 512 devices: a whole 4x4x16 slice. The times are simulated.
512 devices in a mesh: dom: 64 (over x, z), rep: 8 (over y, core).
Axes of the slice: x: 4, y: 4, z: 16, core: 2. Of those that a mesh axis runs over, the one named last changes fastest.
Arguments:
- history: bfloat16 [2, 524288, 256], P(None, ('dom', 'rep')), may hold values from -6 to 6
- tile_values: bfloat16 [4096, 8, 128, 128], P(('dom', 'rep')), may hold values from -0.5 to 0.5
- tile_cols: int32 [4096, 8], P(('dom', 'rep')), may hold values from 0 to 11, all different within a row
- send_rows: int32 [512, 64, 8], P(('dom', 'rep')), may hold values from 0 to 1023
- send_count: int32 [512, 64], P(('dom', 'rep')), may hold values from 1 to 8, as said below
- node_ids: int32 [512, 1024], P(('dom', 'rep')), may hold values from 0 to 1023, each once within a row
- weights: bfloat16 [2, 256, 256], replicated, may hold values from -0.375 to 0.375
- upstream: bfloat16 [524288, 256], P(('dom', 'rep'))
Outputs:
- history_out: bfloat16 [1, 524288, 256], P(None, ('dom', 'rep'))
- weight_grads: float32 [2, 256, 256], replicated
Inputs may be any that keep to these rules, and one draw needn't show every extreme that they name: In each list the first send_count entries are live and the rest empty; in every draw each device has a list of 8 live entries. `tile_cols`: each row block names 8 different column blocks; blocks below 8 hold batch rows, the others halo slots.
All inputs are finite; a program needn't handle non-finite values.
Results may differ from a plain program's by a relative error of at most 0.0065.
Values may be sent and summed in bfloat16 or wider, within the bound.
A program may use at most 64 MiB of HBM per device.

v0:
```python
import math
import jax
import jax.numpy as jnp
from jax import lax
from jax.sharding import PartitionSpec as P

RESTART = 0.1


def layer_beta(level):
    return math.log(0.5 / (level + 1) + 1.0)


def silu_slope(preact):
    sigma = jax.nn.sigmoid(preact)
    return sigma * (1.0 + preact * (1.0 - sigma))


def outgoing(layer_table, send_rows, send_count):
    picked = jnp.take(layer_table, send_rows[0], axis=0)
    slot_index = lax.broadcasted_iota(jnp.int32, send_rows.shape[1:], 1)
    live_mask = slot_index < send_count[0][:, None]
    return jnp.where(live_mask[:, :, None], picked, jnp.zeros_like(picked))


def aggregate(tiles, tile_cols, node_table):
    tile_size = tiles.shape[2]
    blocks = node_table.reshape(-1, tile_size, node_table.shape[1])
    picked = jnp.take(blocks, tile_cols, axis=0)
    summed = jnp.einsum("rtij,rtjf->rif", tiles, picked, preferred_element_type=jnp.float32)
    return summed.reshape(-1, node_table.shape[1])


def spread_back(tiles, tile_cols, back_rows, batch_rows):
    tile_size = tiles.shape[2]
    blocks = back_rows.reshape(-1, tile_size, back_rows.shape[1])
    pieces = jnp.einsum("rtij,rif->rtjf", tiles, blocks, preferred_element_type=jnp.float32)
    targets = lax.broadcasted_iota(jnp.int32, (1, 1, batch_rows // tile_size), 2)
    owners = (tile_cols[:, :, None] == targets).astype(jnp.float32)
    placed = jnp.einsum("rtc,rtjf->cjf", owners, pieces, precision=lax.Precision.HIGHEST)
    return placed.reshape(batch_rows, back_rows.shape[1])


def local(history, tile_values, tile_cols, send_rows, send_count, node_ids, weights, upstream):
    levels = history.shape[0]
    batch_rows = history.shape[1]
    feature_width = history.shape[2]
    node_rows = node_ids[0]
    h_start = jnp.take(history[0], node_rows, axis=0)
    halos = [
        lax.all_to_all(
            outgoing(history[level], send_rows, send_count),
            "dom",
            split_axis=0,
            concat_axis=0,
            tiled=True,
        ).reshape(-1, feature_width)
        for level in range(levels)
    ]
    current = h_start
    mixed_all = []
    preact_all = []
    written = []
    for level in range(levels):
        node_table = jnp.concatenate([current, halos[level]], axis=0)
        summed = aggregate(tile_values, tile_cols, node_table)
        mixed_rows = ((1.0 - RESTART) * summed + RESTART * h_start.astype(jnp.float32)).astype(
            jnp.bfloat16
        )
        beta_value = layer_beta(level)
        preact = (1.0 - beta_value) * mixed_rows.astype(jnp.float32) + beta_value * jnp.dot(
            mixed_rows, weights[level], preferred_element_type=jnp.float32
        )
        current = jax.nn.silu(preact).astype(jnp.bfloat16)
        mixed_all.append(mixed_rows)
        preact_all.append(preact)
        if level + 1 < levels:
            written.append(
                jnp.zeros((batch_rows, feature_width), jnp.bfloat16).at[node_rows].set(current)
            )
    grads = [None] * levels
    grad_rows = (upstream.astype(jnp.float32) * silu_slope(preact_all[-1])).astype(jnp.bfloat16)
    for level in reversed(range(levels)):
        beta_value = layer_beta(level)
        local_grad = beta_value * jnp.dot(
            mixed_all[level].T, grad_rows, preferred_element_type=jnp.float32
        )
        grads[level] = local_grad
        if level > 0:
            back_rows = (
                (1.0 - beta_value) * grad_rows.astype(jnp.float32)
                + beta_value
                * jnp.dot(grad_rows, weights[level].T, preferred_element_type=jnp.float32)
            ).astype(jnp.bfloat16)
            delta = (1.0 - RESTART) * spread_back(tile_values, tile_cols, back_rows, batch_rows)
            grad_rows = (delta * silu_slope(preact_all[level - 1])).astype(jnp.bfloat16)
    stacked = jnp.stack(grads)
    stacked = lax.psum(stacked, ("dom", "rep"))
    nodes_all = batch_rows * lax.axis_size("dom") * lax.axis_size("rep")
    return (jnp.stack(written), stacked * (1.0 / math.sqrt(nodes_all)))


def solution(mesh):
    return jax.shard_map(
        local,
        mesh=mesh,
        in_specs=(
            P(None, ("dom", "rep"), None),
            P(("dom", "rep"), None, None, None),
            P(("dom", "rep"), None),
            P(("dom", "rep"), None, None),
            P(("dom", "rep"), None),
            P(("dom", "rep"), None),
            P(),
            P(("dom", "rep"), None),
        ),
        out_specs=(P(None, ("dom", "rep"), None), P()),
        check_vma=False,
    )
```

profile of v0, /device:TPU:4, one launch (start us, length us, event | category | flops | bytes accessed | tf_op | source)
XLA Modules:
  0.0 560.6 jit_solution(8905946658000197402)
XLA Ops:
  7.2 0.7 compare_and_fusion.1
  7.9 0.7 compare_select_fusion.2
  8.7 0.7 iota_compare_fusion.1
  9.6 1.3 slice_bitcast_fusion
  10.9 2.0 gather_fusion.3
  12.9 2.0 gather_fusion.1
  14.8 1.0 fusion.39
  15.8 18.7 %all-to-all-start = ((bf16[64,8,256]{2,1,0:T(8,128)(2,1)}), bf16[64,8,256]{2,1,0:T(8,128)(2,1)S(1)}, u32[]{:S(2)}, u32[]{:S(2)}) async-start(bf16[64,8,256]{2,1,0:T(8,128)(2,1)} %get-tuple-element.7), calls=%async_computation | async-start | bytes 524288 | tf_op jit(solution)/shard_map/all_to_all | solution.py:51
  34.7 3.9 gather_fusion
  38.6 2.9 copy.20
  41.8 13.6 %all-to-all-done = bf16[64,8,256]{2,1,0:T(8,128)(2,1)S(1)} async-done(((bf16[64,8,256]{2,1,0:T(8,128)(2,1)}), bf16[64,8,256]{2,1,0:T(8,128)(2,1)S(1)}, u32[]{:S(2)}, u32[]{:S(2)}) %all-to-all-start) | async-done | bytes 262176 | tf_op jit(solution)/shard_map/all_to_all | solution.py:51
  55.3 6.8 %all-to-all-start.1 = ((bf16[64,8,256]{2,1,0:T(8,128)(2,1)}), bf16[64,8,256]{2,1,0:T(8,128)(2,1)}, u32[]{:S(2)}, u32[]{:S(2)}) async-start(bf16[64,8,256]{2,1,0:T(8,128)(2,1)} %get-tuple-element.6), calls=%async_computation.1 | async-start | bytes 524288 | tf_op jit(solution)/shard_map/all_to_all | solution.py:51
  62.5 2.8 gather_fusion.2
  65.2 3.0 fusion.38
  68.5 0.8 copy-done.4
  69.3 1.6 multiply_convert_fusion.1
  70.9 11.3 %all-to-all-done.1 = bf16[64,8,256]{2,1,0:T(8,128)(2,1)} async-done(((bf16[64,8,256]{2,1,0:T(8,128)(2,1)}), bf16[64,8,256]{2,1,0:T(8,128)(2,1)}, u32[]{:S(2)}, u32[]{:S(2)}) %all-to-all-start.1) | async-done | bytes 262176 | tf_op jit(solution)/shard_map/all_to_all | solution.py:51
  82.2 1.2 pad_maximum_fusion.1
  83.4 2.8 gather_fusion.4
  86.1 3.0 fusion.37
  89.5 0.7 multiply_convert_fusion
  90.1 0.3 fusion.32
  91.1 1.2 fusion.54
  92.3 5.6 fusion.28
  97.9 0.3 copy.17
  98.2 0.3 fusion.36
  98.6 0.3 copy-done.5
  98.9 0.3 fusion.33
  99.2 0.8 pad_maximum_fusion.2
  100.1 6.1 %scatter_custom_fusion = bf16[1024,256]{1,0:T(8,128)(2,1)} fusion(s32[1024]{0:T(1024)S(1)} %bitcast.119, bf16[1024,256]{1,0:T(8,128)(2,1)} %get-tuple-element.10, bf16[]{:T(256)} %constant.29.clone.1), kind=kCustom, calls=%fused_computation.60 | custom fusion | bytes 524800 | tf_op jit(solution)/shard_map/scatter | solution.py:79
  106.2 445.7 %all-reduce.2.cloned.1.call-done = f32[2,256,256]{2,1,0:T(8,128)} async-done(((f32[2,256,256]{2,1,0:T(8,128)}), f32[2,256,256]{2,1,0:T(8,128)}) %all-reduce.2.cloned.1.call-update) | async-done | bytes 524304 | tf_op jit(solution)/shard_map/psum | solution.py:98
  551.9 1.9 broadcast_multiply_fusion
  (39 shorter events, 2.0 us)
Async XLA Ops:
  9.6 25.0 %copy-start.6 = (s32[8,8]{1,0:T(8,128)S(1)}, s32[8,8]{1,0:T(8,128)}, u32[]{:S(2)}) copy-start(s32[8,8]{1,0:T(8,128)} %param.14) | copy-start | bytes 772
  9.6 25.0 %copy-start.7 = (s32[1,1024]{1,0:T(1,128)S(1)}, s32[1,1024]{1,0:T(1,128)}, u32[]{:S(2)}) copy-start(s32[1,1024]{1,0:T(1,128)} %param.17) | copy-start | bytes 12292
  12.8 25.8 %copy-start = (bf16[8,8,128,128]{3,2,1,0:T(8,128)(2,1)S(1)}, bf16[8,8,128,128]{3,2,1,0:T(8,128)(2,1)}, u32[]{:S(2)}) copy-start(bf16[8,8,128,128]{3,2,1,0:T(8,128)(2,1)} %param.13) | copy-start | bytes 6291460
  15.8 39.5 %all-to-all-start = ((bf16[64,8,256]{2,1,0:T(8,128)(2,1)}), bf16[64,8,256]{2,1,0:T(8,128)(2,1)S(1)}, u32[]{:S(2)}, u32[]{:S(2)}) async-start(bf16[64,8,256]{2,1,0:T(8,128)(2,1)} %get-tuple-element.7), calls=%async_computation | async-start | bytes 524288 | tf_op jit(solution)/shard_map/all_to_all | solution.py:51
  55.3 26.8 %all-to-all-start.1 = ((bf16[64,8,256]{2,1,0:T(8,128)(2,1)}), bf16[64,8,256]{2,1,0:T(8,128)(2,1)}, u32[]{:S(2)}, u32[]{:S(2)}) async-start(bf16[64,8,256]{2,1,0:T(8,128)(2,1)} %get-tuple-element.6), calls=%async_computation.1 | async-start | bytes 524288 | tf_op jit(solution)/shard_map/all_to_all | solution.py:51
  62.2 489.7 %all-reduce.2.cloned.1.call-start = ((), (), s32[]{:S(2)}) async-start(), calls=%async_computation.2 | async-start | bytes 1048576 | tf_op jit(solution)/shard_map/psum | solution.py:98
  62.5 2.8 copy-start.1
  65.2 4.1 copy-start.9
  68.5 0.8 copy-start.4
  86.1 3.3 copy-start.8
  86.1 3.3 copy-start.10
  89.5 1.6 copy-start.2
  92.3 5.9 %copy-start.3 = (f32[1024,256]{1,0:T(8,128)S(1)}, f32[1024,256]{1,0:T(8,128)}, u32[]{:S(2)}) copy-start(f32[1024,256]{1,0:T(8,128)} %get-tuple-element.11) | copy-start | bytes 3145732
  97.9 1.1 copy-start.5
Sparse Core Ops, SparseCore 0:
  100.2 451.6 all-reduce.1
where the time goes:
time: 561 us
  waiting for transfers between devices  471 us (84%)
  local copies, waits for them, and re-layouts  25.8 us (5%)
  starting transfers between devices  25.7 us (5%)
  matrix products  16.1 us (3%)
  between operations  14.3 us (3%)
  other arithmetic  8.14 us (1%)
    psum x1, waiting for transfers between devices, local(): stacked = lax.psum(stacked, ('dom', 'rep'))  446 us
    all_to_all x2, starting transfers between devices, local(): lax.all_to_all(outgoing(history[level], send_rows, send_count), 'dom', sp...  25.5 us
    all_to_all x2, waiting for transfers between devices, local(): lax.all_to_all(outgoing(history[level], send_rows, send_count), 'dom', sp...  24.8 us
  transfers between devices with their start and end apart: 3, of which 3 were waited for; matrix products, arithmetic and copies ran while one was open for 4% of the time, Pallas kernels for 0%

commit v1 on v0

--- a/solution.py
+++ b/solution.py
@@ -5,6 +5,11 @@
 from jax.sharding import PartitionSpec as P
 
 RESTART = 0.1
+
+
+def by_each_axis(array, axis_one, axis_two):
+    inner = lax.psum(array, axis_one)
+    return lax.psum(inner, axis_two)
 
 
 def layer_beta(level):
@@ -95,7 +100,7 @@
             delta = (1.0 - RESTART) * spread_back(tile_values, tile_cols, back_rows, batch_rows)
             grad_rows = (delta * silu_slope(preact_all[level - 1])).astype(jnp.bfloat16)
     stacked = jnp.stack(grads)
-    stacked = lax.psum(stacked, ("dom", "rep"))
+    stacked = by_each_axis(stacked, "dom", "rep")
     nodes_all = batch_rows * lax.axis_size("dom") * lax.axis_size("rep")
     return (jnp.stack(written), stacked * (1.0 / math.sqrt(nodes_all)))
 

time: 561 us -> 441 us (0.79)
  the two profiles are of different devices: /device:TPU:4 before, /device:TPU:2 now
where the time goes in v1:
time: 441 us; the launch traced here: 440 us
  waiting for transfers between devices  350 us (79%)
  starting transfers between devices  25.9 us (6%)
  local copies, waits for them, and re-layouts  25.8 us (6%)
  matrix products  16.1 us (4%)
  between operations  14.3 us (3%)
  other arithmetic  8.13 us (2%)
    psum x1, waiting for transfers between devices, by_each_axis(): inner = lax.psum(array, axis_one)  257 us
    psum x1, waiting for transfers between devices, by_each_axis(): return lax.psum(inner, axis_two)  68.2 us
    all_to_all x2, starting transfers between devices, local(): lax.all_to_all(outgoing(history[level], send_rows, send_count), 'dom', sp...  25.4 us
    all_to_all x2, waiting for transfers between devices, local(): lax.all_to_all(outgoing(history[level], send_rows, send_count), 'dom', sp...  24.9 us
  transfers between devices with their start and end apart: 4, of which 4 were waited for; matrix products, arithmetic and copies ran while one was open for 5% of the time, Pallas kernels for 0%

profile of v1, /device:TPU:2, one launch (start us, length us, event | category | flops | bytes accessed | tf_op | source)
XLA Modules:
  0.0 440.4 jit_solution(16094793235458402484)
XLA Ops:
  7.2 0.7 compare_and_fusion.1
  7.9 0.7 compare_select_fusion.2
  8.7 0.7 iota_compare_fusion.1
  9.6 1.3 slice_bitcast_fusion
  10.9 2.0 gather_fusion.3
  12.9 2.0 gather_fusion.1
  14.8 1.0 fusion.39
  15.8 18.6 %all-to-all-start = ((bf16[64,8,256]{2,1,0:T(8,128)(2,1)}), bf16[64,8,256]{2,1,0:T(8,128)(2,1)S(1)}, u32[]{:S(2)}, u32[]{:S(2)}) async-start(bf16[64,8,256]{2,1,0:T(8,128)(2,1)} %get-tuple-element.7), calls=%async_computation | async-start | bytes 524288 | tf_op jit(solution)/shard_map/all_to_all | solution.py:56
  34.6 3.9 gather_fusion
  38.6 2.9 copy.20
  41.7 13.6 %all-to-all-done = bf16[64,8,256]{2,1,0:T(8,128)(2,1)S(1)} async-done(((bf16[64,8,256]{2,1,0:T(8,128)(2,1)}), bf16[64,8,256]{2,1,0:T(8,128)(2,1)S(1)}, u32[]{:S(2)}, u32[]{:S(2)}) %all-to-all-start) | async-done | bytes 262176 | tf_op jit(solution)/shard_map/all_to_all | solution.py:56
  55.3 6.8 %all-to-all-start.1 = ((bf16[64,8,256]{2,1,0:T(8,128)(2,1)}), bf16[64,8,256]{2,1,0:T(8,128)(2,1)}, u32[]{:S(2)}, u32[]{:S(2)}) async-start(bf16[64,8,256]{2,1,0:T(8,128)(2,1)} %get-tuple-element.6), calls=%async_computation.1 | async-start | bytes 524288 | tf_op jit(solution)/shard_map/all_to_all | solution.py:56
  62.4 2.8 gather_fusion.2
  65.2 3.0 fusion.38
  68.5 0.8 copy-done.4
  69.2 1.6 multiply_convert_fusion.1
  70.9 11.3 %all-to-all-done.1 = bf16[64,8,256]{2,1,0:T(8,128)(2,1)} async-done(((bf16[64,8,256]{2,1,0:T(8,128)(2,1)}), bf16[64,8,256]{2,1,0:T(8,128)(2,1)}, u32[]{:S(2)}, u32[]{:S(2)}) %all-to-all-start.1) | async-done | bytes 262176 | tf_op jit(solution)/shard_map/all_to_all | solution.py:56
  82.1 1.2 pad_maximum_fusion.1
  83.3 2.8 gather_fusion.4
  86.1 3.0 fusion.37
  89.4 0.6 multiply_convert_fusion
  90.1 0.3 fusion.32
  90.4 0.3 fusion.31
  91.0 1.2 fusion.54
  92.2 5.6 %fusion.28 = f32[8,128,256]{2,0,1:T(8,128)S(1)} fusion(f32[8,256,8,128]{1,2,0,3:T(8,128)S(1)} %fusion.54, s32[8,8]{1,0:T(8,128)S(1)} %copy-done.6), kind=kOutput, calls=%fused_computation.27 | convolution fusion | flops 201589248 | bytes 9437440 | tf_op jit(solution)/shard_map/rtc,rtjf->cjf/dot_general | solution.py:45
  97.8 0.3 copy.17
  98.2 0.3 fusion.36
  99.2 0.8 pad_maximum_fusion.2
  100.3 257.0 %all-reduce.3.cloned.1.call-done = f32[2,256,256]{2,1,0:T(8,128)} async-done(((f32[2,256,256]{2,1,0:T(8,128)}), f32[2,256,256]{2,1,0:T(8,128)}) %all-reduce.3.cloned.1.call-update) | async-done | bytes 524304 | tf_op jit(solution)/shard_map/psum | solution.py:11
  357.4 6.1 %scatter_custom_fusion = bf16[1024,256]{1,0:T(8,128)(2,1)} fusion(s32[1024]{0:T(1024)S(1)} %bitcast.119, bf16[1024,256]{1,0:T(8,128)(2,1)} %get-tuple-element.10, bf16[]{:T(256)} %constant.29.clone.1), kind=kCustom, calls=%fused_computation.60 | custom fusion | bytes 524800 | tf_op jit(solution)/shard_map/scatter | solution.py:84
  363.5 68.2 %all-reduce.5.cloned.1.call-done = f32[2,256,256]{2,1,0:T(8,128)} async-done(((f32[2,256,256]{2,1,0:T(8,128)}), f32[2,256,256]{2,1,0:T(8,128)}) %all-reduce.5.cloned.1.call-update) | async-done | bytes 524304 | tf_op jit(solution)/shard_map/psum | solution.py:12
  431.7 1.9 broadcast_multiply_fusion
  (42 shorter events, 2.6 us)
Async XLA Ops:
  9.6 24.9 %copy-start.6 = (s32[8,8]{1,0:T(8,128)S(1)}, s32[8,8]{1,0:T(8,128)}, u32[]{:S(2)}) copy-start(s32[8,8]{1,0:T(8,128)} %param.14) | copy-start | bytes 772
  9.6 25.0 %copy-start.7 = (s32[1,1024]{1,0:T(1,128)S(1)}, s32[1,1024]{1,0:T(1,128)}, u32[]{:S(2)}) copy-start(s32[1,1024]{1,0:T(1,128)} %param.17) | copy-start | bytes 12292
  12.8 25.7 %copy-start = (bf16[8,8,128,128]{3,2,1,0:T(8,128)(2,1)S(1)}, bf16[8,8,128,128]{3,2,1,0:T(8,128)(2,1)}, u32[]{:S(2)}) copy-start(bf16[8,8,128,128]{3,2,1,0:T(8,128)(2,1)} %param.13) | copy-start | bytes 6291460
  15.8 39.5 %all-to-all-start = ((bf16[64,8,256]{2,1,0:T(8,128)(2,1)}), bf16[64,8,256]{2,1,0:T(8,128)(2,1)S(1)}, u32[]{:S(2)}, u32[]{:S(2)}) async-start(bf16[64,8,256]{2,1,0:T(8,128)(2,1)} %get-tuple-element.7), calls=%async_computation | async-start | bytes 524288 | tf_op jit(solution)/shard_map/all_to_all | solution.py:56
  55.3 26.8 %all-to-all-start.1 = ((bf16[64,8,256]{2,1,0:T(8,128)(2,1)}), bf16[64,8,256]{2,1,0:T(8,128)(2,1)}, u32[]{:S(2)}, u32[]{:S(2)}) async-start(bf16[64,8,256]{2,1,0:T(8,128)(2,1)} %get-tuple-element.6), calls=%async_computation.1 | async-start | bytes 524288 | tf_op jit(solution)/shard_map/all_to_all | solution.py:56
  62.1 295.3 %all-reduce.3.cloned.1.call-start = ((), (), s32[]{:S(2)}) async-start(), calls=%async_computation.2 | async-start | bytes 1048576 | tf_op jit(solution)/shard_map/psum | solution.py:11
  62.4 2.8 copy-start.1
  65.2 4.1 copy-start.9
  68.4 0.8 copy-start.4
  86.1 3.3 copy-start.8
  86.1 3.3 copy-start.10
  89.4 1.6 copy-start.2
  92.2 5.9 %copy-start.3 = (f32[1024,256]{1,0:T(8,128)S(1)}, f32[1024,256]{1,0:T(8,128)}, u32[]{:S(2)}) copy-start(f32[1024,256]{1,0:T(8,128)} %get-tuple-element.11) | copy-start | bytes 3145732
  97.8 1.1 copy-start.5
  100.0 331.6 %all-reduce.5.cloned.1.call-start = ((), (), s32[]{:S(2)}) async-start(), calls=%async_computation.3 | async-start | bytes 1048576 | tf_op jit(solution)/shard_map/psum | solution.py:12
Sparse Core Ops, SparseCore 0:
  100.2 257.1 all-reduce.2
  359.8 71.8 all-reduce.4
